TPU v7x, 256 devices: a whole 4x4x8 slice. The times are simulated.
256 devices in a mesh: island: 8 (over y, x_lo), tp: 32 (over x_hi, z, core).
Axes of the slice: x: 4 (x_hi: 2, x_lo: 2; x = x_hi * 2 + x_lo), y: 4, z: 8, core: 2. Of those that a mesh axis runs over, the one named last changes fastest.
Arguments:
- query: bfloat16 [8192, 4096], P('island', 'tp'), may hold values from -5 to 5
- key: bfloat16 [8192, 4096], P('island', 'tp'), may hold values from -5 to 5
- value: bfloat16 [8192, 4096], P('island', 'tp'), may hold values from -6 to 6
- resid: bfloat16 [8192, 4096], P(('island', 'tp')), may hold values from -6 to 6
- w_out: bfloat16 [8, 4096, 4096], P('island', 'tp'), may hold values from -0.09375 to 0.09375
- gain: bfloat16 [8, 4096], P('island'), may hold values from 0.5 to 1.5
- grad_norm: bfloat16 [8192, 4096], P(('island', 'tp')), may hold values from -0.59765625 to 0.59765625
- grad_resid: bfloat16 [8192, 4096], P(('island', 'tp')), may hold values from -0.59765625 to 0.59765625
- moment_one: bfloat16 [8, 4096, 4096], P('island', 'tp'), may hold values from -18 to 18
- moment_two: bfloat16 [8, 4096, 4096], P('island', 'tp'), may hold values from 2 to 50
- delta: bfloat16 [8, 4096, 4096], P('island', 'tp'), may hold values from -0.059814453 to 0.059814453
- global_w: float32 [4096, 4096], P('tp', 'island'), may hold values from -0.09375 to 0.09375
- momentum: float32 [4096, 4096], P('tp', 'island'), may hold values from -0.06 to 0.06
Outputs:
- hidden: bfloat16 [8192, 4096], P(('island', 'tp'))
- grad_query: bfloat16 [8192, 4096], P('island', 'tp')
- grad_key: bfloat16 [8192, 4096], P('island', 'tp')
- grad_value: bfloat16 [8192, 4096], P('island', 'tp')
- new_w_out: bfloat16 [8, 4096, 4096], P('island', 'tp')
- new_moment_one: bfloat16 [8, 4096, 4096], P('island', 'tp')
- new_moment_two: bfloat16 [8, 4096, 4096], P('island', 'tp')
- new_global: float32 [4096, 4096], P('tp', 'island')
- new_momentum: float32 [4096, 4096], P('tp', 'island')
- fragment_params: bfloat16 [4096, 4096], P('tp')
All inputs are finite; a program needn't handle non-finite values.
Results may differ from a plain program's by a relative error of at most 0.03.
Values may be sent and summed in bfloat16 or wider, within the bound.
A program may use at most 128 MiB of HBM per device.

v0:
```python
import jax
import jax.numpy as jnp
from jax import lax
from jax.sharding import PartitionSpec as P

HEAD = 128


def norm_back(hidden, gain_row, grad_norm, grad_resid):
    values = hidden.astype(jnp.float32)
    rstd = lax.rsqrt(jnp.mean(values * values, axis=1, keepdims=True) + 1e-05)
    normed = values * rstd
    scaled = grad_norm.astype(jnp.float32) * gain_row.astype(jnp.float32)[None, :]
    inner = jnp.mean(scaled * normed, axis=1, keepdims=True)
    back = grad_resid.astype(jnp.float32) + rstd * (scaled - normed * inner)
    return back.astype(jnp.bfloat16)


def attend(q_block, keys, values):
    count = q_block.shape[0]
    total = keys.shape[0]
    scores = jnp.einsum(
        "qhd,khd->hqk", q_block, keys, preferred_element_type=jnp.float32
    ) * HEAD ** (-0.5)
    qpos = lax.broadcasted_iota(jnp.int32, (count, total), 0)
    kpos = lax.broadcasted_iota(jnp.int32, (count, total), 1)
    scores = jnp.where((kpos <= qpos)[None], scores, -1e30)
    top = jnp.max(scores, axis=2, keepdims=True)
    expo = jnp.exp(scores - top)
    probs32 = expo / jnp.sum(expo, axis=2, keepdims=True)
    probs = probs32.astype(jnp.bfloat16)
    context = jnp.einsum("hqk,khd->qhd", probs, values, preferred_element_type=jnp.float32).astype(
        jnp.bfloat16
    )
    return (probs32, probs, context)


def outer_step(delta, global_w, momentum):
    total = lax.psum_scatter(
        delta[0].astype(jnp.float32).astype(jnp.bfloat16), "island", scatter_dimension=1, tiled=True
    ).astype(jnp.float32)
    average = total / lax.axis_size("island")
    new_momentum = 0.9 * momentum + average
    new_global = global_w - 0.7 * (average + 0.9 * new_momentum)
    params = lax.all_gather(new_global.astype(jnp.bfloat16), "island", axis=1, tiled=True)
    return (new_global, new_momentum, params)


def inner_step(query, key, value, resid, weight, gain_row, grad_norm, grad_resid):
    rows = resid.shape[0]
    tokens = query.shape[0]
    width = weight.shape[0]
    heads_here = width // HEAD
    queries = query.reshape(tokens, heads_here, HEAD)
    keys = key.reshape(tokens, heads_here, HEAD)
    values = value.reshape(tokens, heads_here, HEAD)
    q_block = queries
    probs32, probs, context = attend(q_block, keys, values)
    summed = lax.psum_scatter(
        jnp.dot(
            context.reshape(rows * lax.axis_size("tp"), width),
            weight,
            preferred_element_type=jnp.float32,
        ).astype(jnp.bfloat16),
        "tp",
        scatter_dimension=0,
        tiled=True,
    ).astype(jnp.float32)
    hidden = (resid.astype(jnp.float32) + summed).astype(jnp.bfloat16)
    grad_hidden = norm_back(hidden, gain_row, grad_norm, grad_resid)
    piece = lax.all_gather(grad_hidden, "tp", axis=0, tiled=True)
    count = piece.shape[0]
    q_block = queries
    probs32, probs, context = attend(q_block, keys, values)
    grad_w = lax.dot_general(
        context.reshape(count, width),
        piece,
        (((0,), (0,)), ((), ())),
        preferred_element_type=jnp.float32,
    )
    grad_ctx = lax.dot_general(
        piece, weight, (((1,), (1,)), ((), ())), preferred_element_type=jnp.float32
    ).astype(jnp.bfloat16)
    grad_ctx = grad_ctx.reshape(count, heads_here, HEAD)
    grad_probs = jnp.einsum("qhd,khd->hqk", grad_ctx, values, preferred_element_type=jnp.float32)
    row_dot = jnp.sum(grad_ctx.astype(jnp.float32) * context.astype(jnp.float32), axis=2).T[
        :, :, None
    ]
    grad_scores = (probs32 * (grad_probs - row_dot)).astype(jnp.bfloat16)
    q_part = jnp.einsum(
        "hqk,khd->qhd", grad_scores, keys, preferred_element_type=jnp.float32
    ) * HEAD ** (-0.5)
    grad_q = q_part.astype(jnp.bfloat16)
    grad_k = jnp.einsum("hqk,qhd->khd", grad_scores, q_block, preferred_element_type=jnp.float32)
    grad_v = jnp.einsum("hqk,qhd->khd", probs, grad_ctx, preferred_element_type=jnp.float32)
    grad_w, grad_q, grad_k, grad_v = (grad_w, grad_q, grad_k, grad_v)
    grad_k = (grad_k * HEAD ** (-0.5)).astype(jnp.bfloat16)
    grad_v = grad_v.astype(jnp.bfloat16)
    return (
        hidden,
        grad_w,
        grad_q.reshape(tokens, width),
        grad_k.reshape(tokens, width),
        grad_v.reshape(tokens, width),
    )


def per_device(
    query,
    key,
    value,
    resid,
    w_out,
    gain,
    grad_norm,
    grad_resid,
    moment_one,
    moment_two,
    delta,
    global_w,
    momentum,
):
    weight = w_out[0]
    new_global, new_momentum, params = outer_step(delta, global_w, momentum)
    hidden, grad_w, grad_q, grad_k, grad_v = inner_step(
        query, key, value, resid, weight, gain[0], grad_norm, grad_resid
    )
    first = 0.9 * moment_one[0].astype(jnp.float32) + 0.1 * grad_w
    second = 0.95 * moment_two[0].astype(jnp.float32) + 0.05 * grad_w * grad_w
    update = first / (1.0 - 0.9**10) / (jnp.sqrt(second / (1.0 - 0.95**10)) + 1e-08)
    new_weight = (weight.astype(jnp.float32) - 0.001 * update).astype(jnp.bfloat16)
    return (
        hidden,
        grad_q,
        grad_k,
        grad_v,
        new_weight[None],
        first.astype(jnp.bfloat16)[None],
        second.astype(jnp.bfloat16)[None],
        new_global,
        new_momentum,
        params,
    )


def solution(mesh):
    return jax.shard_map(
        per_device,
        mesh=mesh,
        in_specs=(
            P("island", "tp"),
            P("island", "tp"),
            P("island", "tp"),
            P(("island", "tp"), None),
            P("island", "tp", None),
            P("island", None),
            P(("island", "tp"), None),
            P(("island", "tp"), None),
            P("island", "tp", None),
            P("island", "tp", None),
            P("island", "tp", None),
            P("tp", "island"),
            P("tp", "island"),
        ),
        out_specs=(
            P(("island", "tp"), None),
            P("island", "tp"),
            P("island", "tp"),
            P("island", "tp"),
            P("island", "tp", None),
            P("island", "tp", None),
            P("island", "tp", None),
            P("tp", "island"),
            P("tp", "island"),
            P("tp", None),
        ),
        check_vma=False,
    )
```

profile of v0, /device:TPU:1, one launch (start us, length us, event | category | flops | bytes accessed | tf_op | source)
XLA Modules:
  0.0 391.4 jit_solution(6152191191436164102)
XLA Ops:
  7.2 0.0 copy-start
  7.2 0.0 reduce-scatter.5.cloned.1.call-start
  7.2 0.7 reduce-scatter.5.cloned.1.call-update
  7.9 0.0 reduce-scatter.3.cloned.1.call-start
  8.0 0.1 copy-done
  8.1 1.7 fusion.2
  9.8 0.5 fusion.1
  10.3 1.4 copy-done.1
  11.8 0.8 convolution_convert_fusion.3
  12.5 0.5 copy-done.4
  13.0 5.6 %convolution_convert_fusion = bf16[1024,4096]{1,0:T(8,128)(2,1)} fusion(bf16[1024,128]{0,1:T(8,128)(2,1)S(1)} %convolution_convert_fusion.3, bf16[1,128,4096]{2,1,0:T(8,128)(2,1)S(1)} %copy-done.4), kind=kOutput, calls=%fused_computation | convolution fusion | flops 1077936128 | bytes 9699328 | tf_op jit(solution)/shard_map/dot_general | solution.py:60
  18.6 0.0 reduce-scatter.3.cloned.1.call-update
  18.6 0.0 all-gather.5.cloned.1.call-start
  18.7 34.5 %reduce-scatter.5.cloned.1.call-done = bf16[128,512]{1,0:T(8,128)(2,1)} async-done(((bf16[128,4096]{1,0:T(8,128)(2,1)}), bf16[128,512]{1,0:T(8,128)(2,1)}) %reduce-scatter.5.cloned.1.call-update) | async-done | bytes 131088 | tf_op jit(solution)/shard_map/reduce_scatter | solution.py:39
  53.2 1.8 fusion.27
  55.1 0.0 all-gather.5.cloned.1.call-update
  55.1 0.2 all-gather.3.cloned.1.call-start
  55.3 155.5 %reduce-scatter.3.cloned.1.call-done = bf16[32,4096]{1,0:T(8,128)(2,1)} async-done(((bf16[1024,4096]{1,0:T(8,128)(2,1)}), bf16[32,4096]{1,0:T(8,128)(2,1)}) %reduce-scatter.3.cloned.1.call-update) | async-done | bytes 262160 | tf_op jit(solution)/shard_map/reduce_scatter | solution.py:59
  210.9 1.2 fusion.23
  212.0 0.3 fusion.18
  212.3 0.9 fusion.22
  213.2 0.0 all-gather.3.cloned.1.call-update
  213.3 41.1 %all-gather.5.cloned.1.call-done = bf16[128,4096]{1,0:T(8,128)(2,1)} async-done(((bf16[128,512]{1,0:T(8,128)(2,1)}), bf16[128,4096]{1,0:T(8,128)(2,1)}) %all-gather.5.cloned.1.call-update) | async-done | bytes 1048592 | tf_op jit(solution)/shard_map/all_gather | solution.py:45
  254.3 109.1 %all-gather.3.cloned.1.call-done = bf16[1024,4096]{1,0:T(8,128)(2,1)} async-done(((bf16[32,4096]{1,0:T(8,128)(2,1)}), bf16[1024,4096]{1,0:T(8,128)(2,1)}) %all-gather.3.cloned.1.call-update) | async-done | bytes 8388624 | tf_op jit(solution)/shard_map/all_gather | solution.py:71
  363.4 6.4 %fusion.24 = (f32[1024]{0:T(1024)S(1)}, bf16[1024,128]{0,1:T(8,128)(2,1)S(1)}) fusion(bf16[1024,128]{0,1:T(8,128)(2,1)S(1)} %convolution_convert_fusion.3, bf16[1024,4096]{1,0:T(8,128)(2,1)} %all-gather.3.cloned.1.call-done, bf16[1,128,4096]{2,1,0:T(8,128)(2,1)S(1)} %copy-done.4), kind=kOutput, calls=%fused_computation.40 | convolution fusion | flops 1074396160 | bytes 9965568 | tf_op jit(solution)/shard_map/dot_general | solution.py:81
  369.8 0.9 multiply_convert_fusion
  370.8 1.5 fusion.4
  372.3 1.4 fusion.5
  373.7 0.9 fusion.7
  374.6 0.8 copy.24
  375.4 8.5 %fusion.9 = (bf16[1,128,4096]{2,1,0:T(8,128)(2,1)}, bf16[1,128,4096]{2,1,0:T(8,128)(2,1)}, bf16[1,128,4096]{2,1,0:T(8,128)(2,1)}) fusion(bf16[1,128,4096]{2,1,0:T(8,128)(2,1)S(1)} %copy-done.12, bf16[1,128,4096]{2,1,0:T(8,128)(2,1)} %param.21, bf16[1,128,4096]{2,1,0:T(8,128)(2,1)S(1)} %copy-done.4, bf16[1024,128]{0,1:T(8,128)(2,1)S(1)} %convolution_convert_fusion.3, ...), kind=kOutput, calls=%fused_computation.22 | convolution fusion | flops 1083703296 | bytes 14942208 | tf_op jit(solution)/shard_map/dot_general | solution.py:75
  383.9 1.0 copy.27
  (29 shorter events, 0.1 us)
Async XLA Ops:
  7.2 1.0 copy-start
  7.2 46.0 %reduce-scatter.5.cloned.1.call-start = ((), (), s32[]{:S(2)}) async-start(), calls=%async_computation.4 | async-start | bytes 1179648 | tf_op jit(solution)/shard_map/reduce_scatter | solution.py:39
  7.9 3.8 copy-start.13
  7.9 202.9 %reduce-scatter.3.cloned.1.call-start = ((), (), s32[]{:S(2)}) async-start(), calls=%async_computation.2 | async-start | bytes 8650752 | tf_op jit(solution)/shard_map/reduce_scatter | solution.py:59
  9.8 2.0 copy-start.1
  11.8 1.2 copy-start.4
  18.6 34.7 %copy-start.7 = (f32[128,512]{1,0:T(8,128)S(1)}, f32[128,512]{1,0:T(8,128)}, u32[]{:S(2)}) copy-start(f32[128,512]{1,0:T(8,128)} %param.24) | copy-start | bytes 786436
  18.6 34.7 %copy-start.8 = (f32[128,512]{1,0:T(8,128)S(1)}, f32[128,512]{1,0:T(8,128)}, u32[]{:S(2)}) copy-start(f32[128,512]{1,0:T(8,128)} %param.25) | copy-start | bytes 786436
  18.6 36.7 %copy-start.11 = (bf16[1,4096]{1,0:T(2,128)(2,1)S(1)}, bf16[1,4096]{1,0:T(2,128)(2,1)}, u32[]{:S(2)}) copy-start(bf16[1,4096]{1,0:T(2,128)(2,1)} %param.18) | copy-start | bytes 24580
  18.6 192.3 %copy-start.10 = (bf16[32,4096]{1,0:T(8,128)(2,1)S(1)}, bf16[32,4096]{1,0:T(8,128)(2,1)}, u32[]{:S(2)}) copy-start(bf16[32,4096]{1,0:T(8,128)(2,1)} %param.16) | copy-start | bytes 786436
  18.6 193.4 %copy-start.5 = (bf16[32,4096]{1,0:T(8,128)(2,1)S(1)}, bf16[32,4096]{1,0:T(8,128)(2,1)}, u32[]{:S(2)}) copy-start(bf16[32,4096]{1,0:T(8,128)(2,1)} %param.19) | copy-start | bytes 786436
  18.6 193.7 %copy-start.9 = (bf16[32,4096]{1,0:T(8,128)(2,1)S(1)}, bf16[32,4096]{1,0:T(8,128)(2,1)}, u32[]{:S(2)}) copy-start(bf16[32,4096]{1,0:T(8,128)(2,1)} %param.20) | copy-start | bytes 786436
  18.6 235.7 %all-gather.5.cloned.1.call-start = ((), (), s32[]{:S(2)}) async-start(), calls=%async_computation.5 | async-start | bytes 1179648 | tf_op jit(solution)/shard_map/all_gather | solution.py:45
  55.1 308.3 %all-gather.3.cloned.1.call-start = ((), (), s32[]{:S(2)}) async-start(), calls=%async_computation.3 | async-start | bytes 8650752 | tf_op jit(solution)/shard_map/all_gather | solution.py:71
  212.0 157.8 %copy-start.3 = (bf16[32,4096]{1,0:T(8,128)(2,1)}, bf16[32,4096]{1,0:T(8,128)(2,1)S(1)}, u32[]{:S(2)}) copy-start(bf16[32,4096]{1,0:T(8,128)(2,1)S(1)} %get-tuple-element.42) | copy-start | bytes 786436
  363.4 6.4 %copy-start.2 = (f32[1024,1024]{0,1:T(8,128)S(1)}, f32[1024,1024]{0,1:T(8,128)}, u32[]{:S(2)}) copy-start(f32[1024,1024]{0,1:T(8,128)} %copy-done.1) | copy-start | bytes 12582916
  370.7 1.5 copy-start.14
  373.7 1.7 copy-start.12
  375.4 8.5 %copy-start.6 = (bf16[128,4096]{1,0:T(8,128)(2,1)S(1)}, bf16[128,4096]{1,0:T(8,128)(2,1)}, u32[]{:S(2)}) copy-start(bf16[128,4096]{1,0:T(8,128)(2,1)} %all-gather.5.cloned.1.call-done) | copy-start | bytes 3145732
Sparse Core Ops, SparseCore 0:
  10.6 42.6 reduce-scatter.4
  57.6 153.1 reduce-scatter.2
  213.2 41.0 all-gather.4
  257.5 105.8 all-gather.2
where the time goes:
time: 392 us; the launch traced here: 391 us
  waiting for transfers between devices  341 us (87%)
  matrix products  27.6 us (7%)
  between operations  13.9 us (4%)
  other arithmetic  4.69 us (1%)
  local copies, waits for them, and re-layouts  3.92 us (1%)
    reduce_scatter x1, waiting for transfers between devices, inner_step(): lax.psum_scatter(jnp.dot(context.reshape(rows * lax.axis_size('tp'), widt...  156 us
    all_gather x1, waiting for transfers between devices, inner_step(): piece = lax.all_gather(grad_hidden, 'tp', axis=0, tiled=True)  109 us
    all_gather x1, waiting for transfers between devices, outer_step(): lax.all_gather(new_global.astype(jnp.bfloat16), 'island', axis=1, tiled=T...  41.1 us
    reduce_scatter x1, waiting for transfers between devices, outer_step(): lax.psum_scatter(delta[0].astype(jnp.float32).astype(jnp.bfloat16), 'isla...  34.5 us
    dot_general x1, matrix products, inner_step(): lax.dot_general(context.reshape(count, width), piece, (((0,), (0,)), ((),...  8.48 us
  transfers between devices with their start and end apart: 4, of which 4 were waited for; matrix products, arithmetic and copies ran while one was open for 3% of the time, Pallas kernels for 0%

commit v1 on v0

v1 whole, which is shorter than its diff:
```python
import functools

import jax
import jax.numpy as jnp
from jax import lax
from jax.experimental import pallas as pl
from jax.experimental.pallas import tpu as pltpu
from jax.sharding import PartitionSpec as P

HEAD = 128
SCALE = HEAD ** (-0.5)
MESH = pl.DeviceIdType.MESH
F32 = jnp.float32
BF16 = jnp.bfloat16
NZ = 8
NY = 4
Q = 1024
R = 32


def f32(a):
    return a.astype(F32)


def dot(a, b):
    return lax.dot_general(a, b, (((1,), (0,)), ((), ())), preferred_element_type=F32)


def dot_nt(a, b):
    return lax.dot_general(a, b, (((1,), (1,)), ((), ())), preferred_element_type=F32)


def dot_tn(a, b):
    return lax.dot_general(a, b, (((0,), (0,)), ((), ())), preferred_element_type=F32)


def kernel(
    q_in, k_in, v_in, resid_in, w_in, gain_ref, gn_in, gr_in, m1_in, m2_in, d_in, gl_in, mo_in,
    hid_out, dq_out, dk_out, dv_out, nw_out, nm1_out, nm2_out, ng_out, nmo_out, par_out,
    q4, kv, vv, w2, wp, res, gnv, grv, m1v, m2v, glv, mov,
    qs, prs, ctx, part, xrecv, rbuf, zbuf, xbuf, fin, hidv, gq, G,
    gco, gcs, gcr, gwacc, gws, gwr, dkacc, dvacc, dqv, dkv, dvv,
    yrecv, hbuf, xlrecv, pbuf, ngv, nmov,
    ld, od, ctx_s, ctx_r, w_s, w_r, xe_s, xe_r, ring_s, ring_r, fin_s, fin_r,
    a0_s, a0_r, ag_s, ag_r, xf_s, xf_r, gc_s, gc_r, gw_s, gw_r,
    ia_s, ia_r, ib_s, ib_r, ic_s, ic_r, id_s, id_r,
):
    isl = lax.axis_index("island")
    tp = lax.axis_index("tp")
    y, xl = isl // 2, lax.rem(isl, 2)
    xh, z, c = tp // 16, lax.rem(tp // 2, NZ), lax.rem(tp, 2)
    oc, oh = 1 - c, 1 - xh

    def tp_dev(a, b, d):
        return (isl, a * 16 + b * 2 + d)

    sib = tp_dev(xh, z, oc)
    opp = tp_dev(oh, z, c)
    opx = tp_dev(oh, z, oc)
    up = tp_dev(xh, lax.rem(z + 1, NZ), c)
    down = tp_dev(xh, lax.rem(z + NZ - 1, NZ), c)
    nxt = (up, down)
    ypeer = [(lax.rem(y + o, NY) * 2 + xl, tp) for o in (1, 2, 3)]
    xlpeer = (y * 2 + 1 - xl, tp)

    def rc(src, dst, ss, rs, dev):
        return pltpu.make_async_remote_copy(
            src_ref=src, dst_ref=dst, send_sem=ss, recv_sem=rs, device_id=dev, device_id_type=MESH
        )

    def cols(ref, at, width):
        return ref.at[:, pl.ds(pl.multiple_of(at * width, width), width)]

    loads = {}

    def load(name, src, dst):
        cp = pltpu.make_async_copy(src, dst, ld.at[len(loads)])
        loads[name] = cp
        cp.start()

    load("q", q_in, q4)
    load("k", k_in, kv)
    load("v", v_in, vv)
    load("wp", cols(w_in, c, 2048), wp.at[0])

    barrier = pltpu.get_barrier_semaphore()
    partners = [sib, opp, opx, up, down, xlpeer] + ypeer
    for dev in partners:
        pl.semaphore_signal(barrier, inc=1, device_id=dev, device_id_type=MESH)
    pl.semaphore_wait(barrier, len(partners))

    w_copy = rc(cols(w_in, oc, 2048), wp.at[1], w_s, w_r, sib)
    w_copy.start()

    a_copies = []
    for o in range(3):
        ny = lax.rem(y + o + 1, NY)
        for e in range(2):
            cp = rc(cols(d_in, ny * 2 + e, 512), yrecv.at[y, e], ia_s.at[o, e], ia_r.at[o, e], ypeer[o])
            cp.start()
            a_copies.append(cp)
    for e in range(2):
        load(f"d{e}", cols(d_in, y * 2 + e, 512), yrecv.at[y, e])
    for e in range(2):
        load(f"res{e}", resid_in.at[:, e * 2048 : (e + 1) * 2048], res.at[e])
        load(f"gn{e}", gn_in.at[:, e * 2048 : (e + 1) * 2048], gnv.at[e])
        load(f"gr{e}", gr_in.at[:, e * 2048 : (e + 1) * 2048], grv.at[e])
    load("gl", gl_in, glv)
    load("mo", mo_in, mov)
    for e in range(2):
        load(f"w{e}", w_in.at[:, e * 2048 : (e + 1) * 2048], w2.at[e])
        load(f"m1{e}", m1_in.at[:, e * 2048 : (e + 1) * 2048], m1v.at[e])
        load(f"m2{e}", m2_in.at[:, e * 2048 : (e + 1) * 2048], m2v.at[e])

    def places(g):
        return lax.rem(z - g + NZ, NZ), lax.rem(z + g, NZ)

    def ctx_copy(g):
        return rc(ctx.at[g, 0], ctx.at[g, 1], ctx_s.at[g], ctx_r.at[g], sib)

    def xe_copy(g):
        return rc(part.at[g, 1, oh], xrecv.at[g], xe_s.at[g], xe_r.at[g], opp)

    def attend(g):
        s0, s1 = places(g)
        qu = jnp.concatenate([q4[0, s0, 0], q4[0, s1, 1], q4[1, s0, 0], q4[1, s1, 1]], axis=0)
        qs[g] = qu
        scores = dot_nt(qu, kv[...]) * SCALE
        row = lax.broadcasted_iota(jnp.int32, (4 * R, 1), 0)
        odd = lax.rem(row // R, 2)
        qpos = (row // (2 * R)) * 512 + odd * R + lax.rem(row, R) + 64 * (s0 + odd * (s1 - s0))
        kpos = lax.broadcasted_iota(jnp.int32, (4 * R, 1024), 1)
        scores = jnp.where(kpos <= qpos, scores, -1e30)
        expo = jnp.exp(scores - jnp.max(scores, axis=1, keepdims=True))
        probs = (expo * (1.0 / jnp.sum(expo, axis=1, keepdims=True))).astype(BF16)
        prs[g] = probs
        ctx[g, 0] = dot(probs, vv[...]).astype(BF16)
        ctx_copy(g).start()

    def both(g):
        return jnp.concatenate([ctx[g, 0], ctx[g, 1]], axis=1)

    def project(g):
        ctx_copy(g).wait_recv()
        cx = both(g)
        for t in (1, 0):
            wt = wp[:, :, t * Q : (t + 1) * Q].reshape(256, Q)
            part[g, t] = dot(cx, wt).astype(BF16).reshape(2, 2, R, Q)
            if t == 1:
                xe_copy(g).start()

    def ring_copy(k, p, j):
        src = part.at[k + 1, 0, j, p] if j < 2 else part.at[k + 1, 1, xh, p]
        return rc(src, rbuf.at[k, p, j], ring_s.at[k, p, j], ring_r.at[k, p, j], nxt[p])

    def z_step(k, first=False):
        for h in range(2):
            for p in range(2):
                if not first:
                    ring_copy(k - 1, p, h).wait_recv()
                    part[k + 1, 0, h, p] = (
                        f32(part[k + 1, 0, h, p]) + f32(rbuf[k - 1, p, h])
                    ).astype(BF16)
                ring_copy(k, p, h).start()

    def x_step(k, first=False):
        xe_copy(k + 1).wait_recv()
        for p in range(2):
            total = f32(part[k + 1, 1, xh, p]) + f32(xrecv[k + 1, p])
            if not first:
                ring_copy(k - 1, p, 2).wait_recv()
                total = total + f32(rbuf[k - 1, p, 2])
            part[k + 1, 1, xh, p] = total.astype(BF16)
            ring_copy(k, p, 2).start()

    ib_copy = rc(hbuf, xlrecv, ib_s, ib_r, xlpeer)
    ic_copy = rc(pbuf.at[y, xl], pbuf.at[y, xl], ic_s, ic_r, xlpeer)
    id_copies = [rc(pbuf.at[y], pbuf.at[y], id_s.at[o], id_r.at[o], ypeer[o]) for o in range(3)]

    def over_y(e):
        return f32(yrecv[0, e]) + f32(yrecv[1, e]) + f32(yrecv[2, e]) + f32(yrecv[3, e])

    def outer_b():
        for cp in a_copies:
            cp.wait_recv()
        loads["d0"].wait()
        loads["d1"].wait()
        hbuf[...] = over_y(1 - xl).astype(BF16)
        ib_copy.start()

    def outer_c():
        ib_copy.wait_recv()
        loads["gl"].wait()
        loads["mo"].wait()
        average = (over_y(xl) + f32(xlrecv[...])) * 0.125
        moment = 0.9 * mov[...] + average
        new = glv[...] - 0.7 * (average + 0.9 * moment)
        nmov[...] = moment
        ngv[...] = new
        pbuf[y, xl] = new.astype(BF16)
        ic_copy.start()

    def outer_d():
        ic_copy.wait_recv()
        for cp in id_copies:
            cp.start()

    loads["q"].wait()
    loads["k"].wait()
    loads["v"].wait()
    attend(1)
    attend(2)
    loads["wp"].wait()
    w_copy.wait_recv()
    project(1)
    z_step(0, first=True)
    attend(3)
    project(2)
    project(3)
    x_step(0, first=True)

    def forward(k, carry):
        z_step(k)
        x_step(k)

        @pl.when(k <= 5)
        def _():
            g = lax.rem(k + 3, NZ)
            attend(g)
            project(g)

        @pl.when(k == 3)
        def _():
            outer_b()

        @pl.when(k == 5)
        def _():
            outer_c()

        return carry

    lax.fori_loop(1, 7, forward, 0)

    fin_copies = [
        rc(zbuf.at[xh, oc], fin.at[0], fin_s.at[0], fin_r.at[0], sib),
        rc(zbuf.at[oh, c], fin.at[1], fin_s.at[1], fin_r.at[1], opp),
        rc(zbuf.at[oh, oc], fin.at[2], fin_s.at[2], fin_r.at[2], opx),
        rc(xbuf.at[oc], fin.at[3], fin_s.at[3], fin_r.at[3], sib),
    ]
    for h in range(2):
        for p in range(2):
            ring_copy(6, p, h).wait_recv()
            zbuf[h, p] = (f32(part[0, 0, h, p]) + f32(rbuf[6, p, h])).astype(BF16)
    for i in (1, 2, 0):
        fin_copies[i].start()
    xe_copy(0).wait_recv()
    for p in range(2):
        ring_copy(6, p, 2).wait_recv()
        xbuf[p] = (f32(part[0, 1, xh, p]) + f32(xrecv[0, p]) + f32(rbuf[6, p, 2])).astype(BF16)
    fin_copies[3].start()
    for e in range(2):
        for name in ("res", "gn", "gr"):
            loads[f"{name}{e}"].wait()
    fin_copies[0].wait_recv()
    fin_copies[3].wait_recv()
    fin_copies[1].wait_recv()
    fin_copies[2].wait_recv()

    def of_block(cc, t):
        if t == 0:
            if cc is c:
                return f32(zbuf[xh, c]) + f32(fin[1])
            return f32(fin[0]) + f32(fin[2])
        return f32(xbuf[c]) if cc is c else f32(fin[3])

    blocks = [(cc, t) for cc in (c, oc) for t in range(2)]
    gain_low, gain_high = gain_ref[:, :2048], gain_ref[:, 2048:]
    low = c == 0
    values, scaleds = [], []
    square = jnp.zeros((R, 1), F32)
    cross = jnp.zeros((R, 1), F32)
    for cc, t in blocks:
        at = slice(t * Q, (t + 1) * Q)
        hid = (f32(res[cc, :, at]) + of_block(cc, t)).astype(BF16)
        hidv[cc, :, at] = hid
        val = f32(hid)
        first_half = low if cc is c else jnp.logical_not(low)
        gain = jnp.where(first_half, f32(gain_low[:, at]), f32(gain_high[:, at]))
        scaled = f32(gnv[cc, :, at]) * gain
        square = square + jnp.sum(val * val, axis=1, keepdims=True)
        cross = cross + jnp.sum(scaled * val, axis=1, keepdims=True)
        values.append(val)
        scaleds.append(scaled)
    rstd = lax.rsqrt(square * (1.0 / 4096) + 1e-05)
    inner = cross * rstd * (1.0 / 4096)
    for (cc, t), val, scaled in zip(blocks, values, scaleds):
        at = slice(t * Q, (t + 1) * Q)
        back = f32(grv[cc, :, at]) + rstd * (scaled - val * rstd * inner)
        gq[cc, t] = back.astype(BF16)
    a0_copies = [
        rc(gq.at[c, 0], G.at[0, 0, xh, c], a0_s.at[2], a0_r.at[2], opp),
        rc(gq.at[oc, 0], G.at[0, 0, xh, c], a0_s.at[3], a0_r.at[3], opx),
        rc(gq.at[oc, 0], G.at[0, 0, xh, c], a0_s.at[0], a0_r.at[0], sib),
        rc(gq.at[oc, 1], G.at[0, 1, xh, c], a0_s.at[1], a0_r.at[1], sib),
    ]
    for cp in a0_copies:
        cp.start()
    for t in range(2):
        G[0, t, xh, c] = gq[c, t]
    gwacc[...] = jnp.zeros_like(gwacc)
    dkacc[...] = jnp.zeros_like(dkacc)
    dvacc[...] = jnp.zeros_like(dvacc)

    outs = []

    def emit(src, dst):
        cp = pltpu.make_async_copy(src, dst, od.at[len(outs)])
        outs.append(cp)
        cp.start()

    for e in range(2):
        emit(hidv.at[e], hid_out.at[:, e * 2048 : (e + 1) * 2048])
    emit(ngv, ng_out)
    emit(nmov, nmo_out)

    def ag_copy(k, p, j):
        t, h = (0, j) if j < 2 else (1, xh)
        return rc(
            G.at[k, t, h, p], G.at[k + 1, t, h, p], ag_s.at[k, p, j], ag_r.at[k, p, j], nxt[p]
        )

    def xf_copy(g, p):
        return rc(G.at[g, 1, xh, p], G.at[g, 1, xh, p], xf_s.at[g, p], xf_r.at[g, p], opp)

    for cp in (a0_copies[2], a0_copies[3], a0_copies[0], a0_copies[1]):
        cp.wait_recv()
    for j in (2, 0, 1):
        for p in range(2):
            ag_copy(0, p, j).start()
            if j == 2:
                xf_copy(0, p).start()

    def weigh(g):
        for p in range(2):
            xf_copy(g, p).wait_recv()
        gc = None
        cx = both(g)
        for t in range(2):
            gt = G[g, t].reshape(4 * R, Q)
            wt = wp[:, :, t * Q : (t + 1) * Q].reshape(256, Q)
            piece = dot_nt(gt, wt)
            gc = piece if gc is None else gc + piece
        gco[g] = gc[:, :HEAD]
        gcs[g] = gc[:, HEAD:]
        gc_copy(g).start()
        for t in range(2):
            gt = G[g, t].reshape(4 * R, Q)
            gwacc[:, t * Q : (t + 1) * Q] += dot_tn(cx, gt)

    def gc_copy(g):
        return rc(gcs.at[g], gcr.at[g], gc_s.at[g], gc_r.at[g], sib)

    def attend_back(g):
        gc_copy(g).wait_recv()
        s0, s1 = places(g)
        gc = (gco[g] + gcr[g]).astype(BF16)
        probs = prs[g]
        row_dot = jnp.sum(f32(gc) * f32(ctx[g, 0]), axis=1, keepdims=True)
        gs = (f32(probs) * (dot_nt(gc, vv[...]) - row_dot)).astype(BF16)
        dq = (dot(gs, kv[...]) * SCALE).astype(BF16)
        for h in range(2):
            for p, s in enumerate((s0, s1)):
                dqv[h, s, p] = dq[(2 * h + p) * R : (2 * h + p + 1) * R]
        dkacc[...] += dot_tn(gs, qs[g])
        dvacc[...] += dot_tn(probs, gc)

    def backward(k, carry):
        for j in (2, 0, 1):
            for p in range(2):
                ag_copy(k, p, j).wait_recv()

                @pl.when(k < 6)
                def _():
                    ag_copy(k + 1, p, j).start()

                if j == 2:
                    xf_copy(k + 1, p).start()

        weigh(k)

        @pl.when(k >= 1)
        def _():
            attend_back(k - 1)

        @pl.when(k == 1)
        def _():
            outer_d()

        return carry

    lax.fori_loop(0, 7, backward, 0)

    weigh(7)
    gws[...] = gwacc[HEAD:].astype(BF16)
    gw_copy = rc(gws, gwr, gw_s, gw_r, sib)
    gw_copy.start()
    attend_back(6)
    attend_back(7)
    dkv[...] = (dkacc[...] * SCALE).astype(BF16)
    dvv[...] = dvacc[...].astype(BF16)
    emit(dqv, dq_out)
    emit(dkv, dk_out)
    emit(dvv, dv_out)
    for cp in id_copies:
        cp.wait_recv()
    for i in range(8):
        emit(pbuf.at[i // 2, i % 2], par_out.at[:, i * 512 : (i + 1) * 512])

    for e in range(2):
        for name in ("w", "m1", "m2"):
            loads[f"{name}{e}"].wait()

    def adam(cc, grad_of):
        for i in range(8):
            rows = slice(i * 16, (i + 1) * 16)
            grad = grad_of(rows)
            first = 0.9 * f32(m1v[cc, rows]) + 0.1 * grad
            second = 0.95 * f32(m2v[cc, rows]) + 0.05 * grad * grad
            update = (first * (1.0 / (1.0 - 0.9**10))) / (
                jnp.sqrt(second * (1.0 / (1.0 - 0.95**10))) + 1e-08
            )
            w2[cc, rows] = (f32(w2[cc, rows]) - 0.001 * update).astype(BF16)
            m1v[cc, rows] = first.astype(BF16)
            m2v[cc, rows] = second.astype(BF16)
        for src, dst in ((w2, nw_out), (m1v, nm1_out), (m2v, nm2_out)):
            emit(src.at[cc], cols(dst, cc, 2048))

    adam(c, lambda rows: gwacc[rows])
    gw_copy.wait_recv()
    adam(oc, lambda rows: f32(gwr[rows]))

    w_copy.wait_send()
    gw_copy.wait_send()
    for cp in a_copies + fin_copies + a0_copies + id_copies + [ib_copy, ic_copy]:
        cp.wait_send()

    def drain8(g, carry):
        ctx_copy(g).wait_send()
        xe_copy(g).wait_send()
        gc_copy(g).wait_send()
        for p in range(2):
            xf_copy(g, p).wait_send()
        return carry

    lax.fori_loop(0, 8, drain8, 0)

    def drain7(k, carry):
        for p in range(2):
            for j in range(3):
                ring_copy(k, p, j).wait_send()
                ag_copy(k, p, j).wait_send()
        return carry

    lax.fori_loop(0, 7, drain7, 0)
    for cp in outs:
        cp.wait()


def per_device(
    query, key, value, resid, w_out, gain, grad_norm, grad_resid, moment_one, moment_two,
    delta, global_w, momentum,
):
    any_spec = pl.BlockSpec(memory_space=pl.ANY)
    dma = pltpu.SemaphoreType.DMA

    def vm(shape, dtype=BF16):
        return pltpu.VMEM(shape, dtype)

    def shape(dims, dtype=BF16):
        return jax.ShapeDtypeStruct(dims, dtype)

    scratch = [
        vm((2, 8, 2, R, HEAD)), vm((1024, HEAD)), vm((1024, HEAD)), vm((2, 128, 2048)),
        vm((2, 128, 2048)), vm((2, R, 2048)), vm((2, R, 2048)), vm((2, R, 2048)),
        vm((2, 128, 2048)), vm((2, 128, 2048)), vm((128, 512), F32), vm((128, 512), F32),
        vm((8, 128, HEAD)), vm((8, 128, 1024)), vm((8, 2, 128, HEAD)),
        vm((8, 2, 2, 2, R, Q)), vm((8, 2, R, Q)), vm((7, 2, 3, R, Q)),
        vm((2, 2, R, Q)), vm((2, R, Q)), vm((4, R, Q)),
        vm((2, R, 2048)), vm((2, 2, R, Q)), vm((8, 2, 2, 2, R, Q)),
        vm((8, 128, HEAD), F32), vm((8, 128, HEAD), F32), vm((8, 128, HEAD), F32),
        vm((256, 2048), F32), vm((128, 2048)), vm((128, 2048)),
        vm((1024, HEAD), F32), vm((1024, HEAD), F32),
        vm((2, 8, 2, R, HEAD)), vm((1024, HEAD)), vm((1024, HEAD)),
        vm((4, 2, 128, 512)), vm((128, 512)), vm((128, 512)), vm((4, 2, 128, 512)),
        vm((128, 512), F32), vm((128, 512), F32),
        dma((20,)), dma((24,)), dma((8,)), dma((8,)), dma, dma,
        dma((8,)), dma((8,)), dma((7, 2, 3)), dma((7, 2, 3)),
        dma((4,)), dma((4,)), dma((4,)), dma((4,)),
        dma((7, 2, 3)), dma((7, 2, 3)), dma((8, 2)), dma((8, 2)),
        dma((8,)), dma((8,)), dma, dma,
        dma((3, 2)), dma((3, 2)), dma, dma, dma, dma, dma((3,)), dma((3,)),
    ]
    hidden, dq, dk, dv, nw, nm1, nm2, ng, nmo, par = pl.pallas_call(
        kernel,
        out_shape=[
            shape((R, 4096)), shape((2, 8, 2, R, HEAD)), shape((1024, HEAD)), shape((1024, HEAD)),
            shape((128, 4096)), shape((128, 4096)), shape((128, 4096)),
            shape((128, 512), F32), shape((128, 512), F32), shape((128, 4096)),
        ],
        in_specs=[any_spec] * 5 + [pl.BlockSpec(memory_space=pltpu.VMEM)] + [any_spec] * 7,
        out_specs=[any_spec] * 10,
        scratch_shapes=scratch,
        compiler_params=pltpu.CompilerParams(
            collective_id=0, has_side_effects=True, vmem_limit_bytes=58 << 20
        ),
        cost_estimate=pl.CostEstimate(flops=5 * 10**9, bytes_accessed=12 << 20, transcendentals=10**6),
        name="whole_step",
    )(
        query.reshape(2, 8, 2, R, HEAD), key, value, resid, w_out[0], gain, grad_norm, grad_resid,
        moment_one[0], moment_two[0], delta[0], global_w, momentum,
    )
    return (
        hidden, dq.reshape(1024, HEAD), dk, dv, nw[None], nm1[None], nm2[None], ng, nmo, par,
    )


def solution(mesh):
    return jax.shard_map(
        per_device,
        mesh=mesh,
        in_specs=(
            P("island", "tp"),
            P("island", "tp"),
            P("island", "tp"),
            P(("island", "tp"), None),
            P("island", "tp", None),
            P("island", None),
            P(("island", "tp"), None),
            P(("island", "tp"), None),
            P("island", "tp", None),
            P("island", "tp", None),
            P("island", "tp", None),
            P("tp", "island"),
            P("tp", "island"),
        ),
        out_specs=(
            P(("island", "tp"), None),
            P("island", "tp"),
            P("island", "tp"),
            P("island", "tp"),
            P("island", "tp", None),
            P("island", "tp", None),
            P("island", "tp", None),
            P("tp", "island"),
            P("tp", "island"),
            P("tp", None),
        ),
        check_vma=False,
    )
```

time: 392 us -> 116 us (0.30)
  waiting for transfers between devices: 341 us -> 0 us
  Pallas kernels: 0 us -> 102 us
  matrix products: 27.6 us -> 0 us
  between operations: 13.9 us -> 0.68 us
  local copies, waits for them, and re-layouts: 3.92 us -> 12.2 us
  other arithmetic: 4.69 us -> 0 us
    reduce_scatter x2 -> x0, waiting for transfers between devices: 190 us -> none  [the longest x1 156 us: inner_step(): lax.psum_scatter(jnp.dot(context.reshape(rows * lax.axis_size('tp'), widt...]
    all_gather x2 -> x0, waiting for transfers between devices: 150 us -> none  [the longest x1 109 us: inner_step(): piece = lax.all_gather(grad_hidden, 'tp', axis=0, tiled=True)]
    pallas_call x0 -> x1, Pallas kernels: none -> 102 us  [per_device(): pl.pallas_call(kernel, out_shape=[shape((R, 4096)), shape((2, 8, 2, R, HE...]
    dot_general x9 -> x0, matrix products: 27.6 us -> none  [the longest x1 8.48 us: inner_step(): lax.dot_general(context.reshape(count, width), piece, (((0,), (0,)), ((),...]
    unnamed x32 -> x26, local copies, waits for them, and re-layouts: 3.92 us -> 12.2 us
  transfers between devices with their start and end apart: 4 -> 0, of which waited for: 4 -> 0; matrix products, arithmetic and copies ran while one was open for 3% -> 0% of each run, Pallas kernels for 0% -> 0%
where the time goes in v1:
time: 116 us; the launch traced here: 115 us
  Pallas kernels  102 us (88%)
  local copies, waits for them, and re-layouts  12.2 us (11%)
    pallas_call x1, Pallas kernels, per_device(): pl.pallas_call(kernel, out_shape=[shape((R, 4096)), shape((2, 8, 2, R, HE...  102 us
    unnamed x26, local copies, waits for them, and re-layouts  12.2 us

profile of v1, /device:TPU:1, one launch (start us, length us, event | category | flops | bytes accessed | tf_op | source)
XLA Modules:
  0.0 115.4 jit_solution(7715300327812929658)
XLA Ops:
  0.6 102.5 %whole_step.1 = (bf16[32,4096]{1,0:T(8,128)(2,1)}, bf16[2,8,2,32,128]{4,3,2,1,0:T(8,128)(2,1)}, bf16[1024,128]{1,0:T(8,128)(2,1)}, bf16[1024,128]{1,0:T(8,128)(2...) custom-call(bf16[2,8,2,32,128]{4,3,2,1,0:T(8,128)(2,1)} %bitcast.17,, ...), custom_call_target="tpu_custom_call" | custom-call | flops 5000000000 | bytes 12582912 | tf_op jit(solution)/shard_map/whole_step/pallas_call | solution.py:503
  103.1 0.0 copy-start.7
  103.2 0.0 copy-start.3
  103.2 1.8 %copy.33 = bf16[32,4096]{1,0:T(8,128)(2,1)} copy(bf16[32,4096]{1,0:T(8,128)(2,1)} %get-tuple-element.40) | data formatting | bytes 524288
  104.9 1.7 %copy.34 = bf16[1024,128]{1,0:T(8,128)(2,1)} copy(bf16[1024,128]{1,0:T(8,128)(2,1)} %bitcast.12) | data formatting | bytes 524288
  106.6 0.0 copy-done.7
  106.6 0.0 copy-start.6
  106.6 0.7 copy.35
  107.3 0.3 copy-done.6
  107.7 0.7 copy.36
  108.4 0.0 copy-done.3
  108.4 0.0 copy-start.2
  108.4 1.0 copy.37
  109.3 0.6 copy-done.2
  110.0 0.0 copy-start.1
  110.0 1.0 copy.38
  110.9 0.6 copy-done.1
  111.6 0.0 copy-start.5
  111.6 0.0 copy-start
  111.6 1.0 copy.39
  112.5 0.1 copy-done.5
  112.7 0.0 copy-start.4
  112.7 0.7 copy.40
  113.4 0.3 copy-done.4
  113.7 0.7 copy.41
  114.4 0.0 copy-done
  114.4 1.0 copy.42
Async XLA Ops:
  103.1 3.5 %copy-start.7 = (bf16[1024,128]{1,0:T(8,128)(2,1)S(1)}, bf16[1024,128]{1,0:T(8,128)(2,1)}, u32[]{:S(2)}) copy-start(bf16[1024,128]{1,0:T(8,128)(2,1)} %get-tuple-element.42) | copy-start | bytes 786436
  103.2 5.2 %copy-start.3 = (bf16[128,4096]{1,0:T(8,128)(2,1)S(1)}, bf16[128,4096]{1,0:T(8,128)(2,1)}, u32[]{:S(2)}) copy-start(bf16[128,4096]{1,0:T(8,128)(2,1)} %get-tuple-element.24) | copy-start | bytes 3145732
  106.6 1.0 copy-start.6
  108.4 1.6 %copy-start.2 = (bf16[128,4096]{1,0:T(8,128)(2,1)S(1)}, bf16[128,4096]{1,0:T(8,128)(2,1)}, u32[]{:S(2)}) copy-start(bf16[128,4096]{1,0:T(8,128)(2,1)} %get-tuple-element.25) | copy-start | bytes 3145732
  110.0 1.6 %copy-start.1 = (bf16[128,4096]{1,0:T(8,128)(2,1)S(1)}, bf16[128,4096]{1,0:T(8,128)(2,1)}, u32[]{:S(2)}) copy-start(bf16[128,4096]{1,0:T(8,128)(2,1)} %get-tuple-element.26) | copy-start | bytes 3145732
  111.6 1.1 copy-start.5
  111.6 2.8 %copy-start = (bf16[128,4096]{1,0:T(8,128)(2,1)S(1)}, bf16[128,4096]{1,0:T(8,128)(2,1)}, u32[]{:S(2)}) copy-start(bf16[128,4096]{1,0:T(8,128)(2,1)} %get-tuple-element.49) | copy-start | bytes 3145732
  112.7 1.0 copy-start.4

commit v2 on v1

v2 whole, which is shorter than its diff:
```python
import functools

import jax
import jax.numpy as jnp
from jax import lax
from jax.experimental import pallas as pl
from jax.experimental.pallas import tpu as pltpu
from jax.sharding import PartitionSpec as P

HEAD = 128
SCALE = HEAD ** (-0.5)
MESH = pl.DeviceIdType.MESH
F32 = jnp.float32
BF16 = jnp.bfloat16
NZ = 8
NY = 4
QZ = 896
QX = 2048 - QZ
SPAN = (slice(0, QZ), slice(QZ, 2048))
R = 32


def f32(a):
    return a.astype(F32)


def dot(a, b):
    return lax.dot_general(a, b, (((1,), (0,)), ((), ())), preferred_element_type=F32)


def dot_nt(a, b):
    return lax.dot_general(a, b, (((1,), (1,)), ((), ())), preferred_element_type=F32)


def dot_tn(a, b):
    return lax.dot_general(a, b, (((0,), (0,)), ((), ())), preferred_element_type=F32)


def kernel(
    q_in, k_in, v_in, resid_in, w_in, gain_ref, gn_in, gr_in, d_in, gl_in, mo_in,
    hid_out, dq_out, dk_out, dv_out, ng_out, nmo_out, par_out, gw_out,
    q4, kv, vv, wp, res, gnv, grv, glv, mov,
    qs, prs, ctx, part0, part1, xrecv, rbuf0, rbuf1, zbuf, xbuf, fin0, fin1, gq0, gq1, G0, G1,
    gco, gcs, gcr, gwacc, gws, gwo, dkacc, dvacc, yrecv, hbuf, xlrecv,
    hidv, dqv, dkv, dvv, ngv, nmov, pbuf,
    ld, od, ctx_s, ctx_r, w_s, w_r, xe_s, xe_r, ring_s, ring_r, fin_s, fin_r,
    a0_s, a0_r, ag_s, ag_r, xf_s, xf_r, gc_s, gc_r, gw_s, gw_r,
    ia_s, ia_r, ib_s, ib_r, ic_s, ic_r, id_s, id_r,
):
    isl = lax.axis_index("island")
    tp = lax.axis_index("tp")
    y, xl = isl // 2, lax.rem(isl, 2)
    xh, z, c = tp // 16, lax.rem(tp // 2, NZ), lax.rem(tp, 2)
    oc, oh = 1 - c, 1 - xh

    def tp_dev(a, b, d):
        return (isl, a * 16 + b * 2 + d)

    sib = tp_dev(xh, z, oc)
    opp = tp_dev(oh, z, c)
    opx = tp_dev(oh, z, oc)
    up = tp_dev(xh, lax.rem(z + 1, NZ), c)
    down = tp_dev(xh, lax.rem(z + NZ - 1, NZ), c)
    nxt = (up, down)
    ypeer = [(lax.rem(y + o, NY) * 2 + xl, tp) for o in (1, 2, 3)]
    xlpeer = (y * 2 + 1 - xl, tp)

    def rc(src, dst, ss, rs, dev):
        return pltpu.make_async_remote_copy(
            src_ref=src, dst_ref=dst, send_sem=ss, recv_sem=rs, device_id=dev, device_id_type=MESH
        )

    def cols(ref, at, width):
        return ref.at[:, pl.ds(pl.multiple_of(at * width, width), width)]

    loads = {}

    def load(name, src, dst):
        cp = pltpu.make_async_copy(src, dst, ld.at[len(loads)])
        loads[name] = cp
        cp.start()

    load("q", q_in, q4)
    load("k", k_in, kv)
    load("v", v_in, vv)
    load("wp", cols(w_in, c, 2048), wp.at[0])

    barrier = pltpu.get_barrier_semaphore()
    partners = [sib, opp, opx, up, down, xlpeer] + ypeer
    for dev in partners:
        pl.semaphore_signal(barrier, inc=1, device_id=dev, device_id_type=MESH)

    def places(g):
        return lax.rem(z - g + NZ, NZ), lax.rem(z + g, NZ)

    def ctx_copy(g):
        return rc(ctx.at[g, 0], ctx.at[g, 1], ctx_s.at[g], ctx_r.at[g], sib)

    def xe_copy(g):
        return rc(part1.at[g, oh], xrecv.at[g], xe_s.at[g], xe_r.at[g], opp)

    def attend(g):
        s0, s1 = places(g)
        qu = jnp.concatenate([q4[0, s0, 0], q4[0, s1, 1], q4[1, s0, 0], q4[1, s1, 1]], axis=0)
        qs[g] = qu
        scores = dot_nt(qu, kv[...]) * SCALE
        row = lax.broadcasted_iota(jnp.int32, (4 * R, 1), 0)
        odd = lax.rem(row // R, 2)
        qpos = (row // (2 * R)) * 512 + odd * R + lax.rem(row, R) + 64 * (s0 + odd * (s1 - s0))
        kpos = lax.broadcasted_iota(jnp.int32, (4 * R, 1024), 1)
        scores = jnp.where(kpos <= qpos, scores, -1e30)
        expo = jnp.exp(scores - jnp.max(scores, axis=1, keepdims=True))
        probs = (expo * (1.0 / jnp.sum(expo, axis=1, keepdims=True))).astype(BF16)
        prs[g] = probs
        ctx[g, 0] = dot(probs, vv[...]).astype(BF16)

    def both(g):
        return jnp.concatenate([ctx[g, 0], ctx[g, 1]], axis=1)

    def project(g, order=(1, 0)):
        ctx_copy(g).wait_recv()
        cx = both(g)
        for t in order:
            wt = wp[:, :, SPAN[t]].reshape(256, -1)
            out = dot(cx, wt).astype(BF16).reshape(2, 2, R, -1)
            if t == 1:
                part1[g] = out
                xe_copy(g).start()
            else:
                part0[g] = out

    halves = (oh, xh, xh)

    def ring_copy(k, p, j):
        if j < 2:
            src, dst = part0.at[k + 1, halves[j], p], rbuf0.at[k, p, j]
        else:
            src, dst = part1.at[k + 1, xh, p], rbuf1.at[k, p]
        return rc(src, dst, ring_s.at[k, p, j], ring_r.at[k, p, j], nxt[p])

    def z_step(k, first=False):
        for j in range(2):
            h = halves[j]
            for p in range(2):
                if not first:
                    ring_copy(k - 1, p, j).wait_recv()
                    part0[k + 1, h, p] = (f32(part0[k + 1, h, p]) + f32(rbuf0[k - 1, p, j])).astype(BF16)
                ring_copy(k, p, j).start()

    def x_step(k, first=False):
        xe_copy(k + 1).wait_recv()
        for p in range(2):
            total = f32(part1[k + 1, xh, p]) + f32(xrecv[k + 1, p])
            if not first:
                ring_copy(k - 1, p, 2).wait_recv()
                total = total + f32(rbuf1[k - 1, p])
            part1[k + 1, xh, p] = total.astype(BF16)
            ring_copy(k, p, 2).start()

    ib_copy = rc(hbuf, xlrecv, ib_s, ib_r, xlpeer)
    ic_copy = rc(pbuf.at[y, xl], pbuf.at[y, xl], ic_s, ic_r, xlpeer)
    id_copies = [rc(pbuf.at[y], pbuf.at[y], id_s.at[o], id_r.at[o], ypeer[o]) for o in range(3)]

    def over_y(e):
        return f32(yrecv[0, e]) + f32(yrecv[1, e]) + f32(yrecv[2, e]) + f32(yrecv[3, e])

    def outer_b():
        for cp in a_copies:
            cp.wait_recv()
        loads["d0"].wait()
        loads["d1"].wait()
        hbuf[...] = over_y(1 - xl).astype(BF16)
        ib_copy.start()

    def outer_c():
        ib_copy.wait_recv()
        loads["gl"].wait()
        loads["mo"].wait()
        average = (over_y(xl) + f32(xlrecv[...])) * 0.125
        moment = 0.9 * mov[...] + average
        new = glv[...] - 0.7 * (average + 0.9 * moment)
        nmov[...] = moment
        ngv[...] = new
        pbuf[y, xl] = new.astype(BF16)
        ic_copy.start()

    def outer_d():
        ic_copy.wait_recv()
        for cp in id_copies:
            cp.start()

    loads["q"].wait()
    loads["k"].wait()
    loads["v"].wait()
    attend(1)
    pl.semaphore_wait(barrier, len(partners))
    w_copy = rc(cols(w_in, oc, 2048), wp.at[1], w_s, w_r, sib)
    w_copy.start()
    ctx_copy(1).start()
    a_copies = []
    for o in range(3):
        ny = lax.rem(y + o + 1, NY)
        for e in range(2):
            cp = rc(cols(d_in, ny * 2 + e, 512), yrecv.at[y, e], ia_s.at[o, e], ia_r.at[o, e], ypeer[o])
            cp.start()
            a_copies.append(cp)
    for e in range(2):
        load(f"d{e}", cols(d_in, y * 2 + e, 512), yrecv.at[y, e])
    for e in range(2):
        load(f"res{e}", resid_in.at[:, e * 2048 : (e + 1) * 2048], res.at[e])
        load(f"gn{e}", gn_in.at[:, e * 2048 : (e + 1) * 2048], gnv.at[e])
        load(f"gr{e}", gr_in.at[:, e * 2048 : (e + 1) * 2048], grv.at[e])
    load("gl", gl_in, glv)
    load("mo", mo_in, mov)
    attend(2)
    ctx_copy(2).start()
    loads["wp"].wait()
    w_copy.wait_recv()
    project(1, order=(0, 1))
    z_step(0, first=True)
    attend(3)
    ctx_copy(3).start()
    project(2)
    project(3)

    def forward_step(k, second=False):
        g = lax.rem(k + 3, NZ)
        z_step(k)
        attend(g)
        ctx_copy(g).start()
        x_step(k - 1, first=second)
        project(g)

    forward_step(1, second=True)

    def forward(k, carry):
        forward_step(k)

        @pl.when(k == 3)
        def _():
            outer_b()

        @pl.when(k == 5)
        def _():
            outer_c()

        return carry

    lax.fori_loop(2, 6, forward, 0)
    z_step(6)
    x_step(5)

    fin_copies = [
        rc(zbuf.at[xh, oc], fin0.at[0], fin_s.at[0], fin_r.at[0], sib),
        rc(zbuf.at[oh, c], fin0.at[1], fin_s.at[1], fin_r.at[1], opp),
        rc(zbuf.at[oh, oc], fin0.at[2], fin_s.at[2], fin_r.at[2], opx),
        rc(xbuf.at[oc], fin1, fin_s.at[3], fin_r.at[3], sib),
    ]

    def z_last(j):
        for p in range(2):
            ring_copy(6, p, j).wait_recv()
            zbuf[halves[j], p] = (f32(part0[0, halves[j], p]) + f32(rbuf0[6, p, j])).astype(BF16)

    z_last(0)
    fin_copies[1].start()
    fin_copies[2].start()
    x_step(6)
    z_last(1)
    fin_copies[0].start()
    xe_copy(0).wait_recv()
    for p in range(2):
        ring_copy(6, p, 2).wait_recv()
        xbuf[p] = (f32(part1[0, xh, p]) + f32(xrecv[0, p]) + f32(rbuf1[6, p])).astype(BF16)
    fin_copies[3].start()
    for e in range(2):
        for name in ("res", "gn", "gr"):
            loads[f"{name}{e}"].wait()
    fin_copies[0].wait_recv()
    fin_copies[3].wait_recv()
    fin_copies[1].wait_recv()
    fin_copies[2].wait_recv()

    def of_block(cc, t):
        if t == 0:
            if cc is c:
                return f32(zbuf[xh, c]) + f32(fin0[1])
            return f32(fin0[0]) + f32(fin0[2])
        return f32(xbuf[c]) if cc is c else f32(fin1[...])

    blocks = [(oc, 1), (oc, 0), (c, 0), (c, 1)]
    low = c == 0
    values, scaleds = [], []
    square = jnp.zeros((R, 1), F32)
    cross = jnp.zeros((R, 1), F32)
    for cc, t in blocks:
        at = SPAN[t]
        hid = (f32(res[cc, :, at]) + of_block(cc, t)).astype(BF16)
        hidv[cc, :, at] = hid
        val = f32(hid)
        first_half = low if cc is c else jnp.logical_not(low)
        gain = jnp.where(
            first_half, f32(gain_ref[:, at]), f32(gain_ref[:, at.start + 2048 : at.stop + 2048])
        )
        scaled = f32(gnv[cc, :, at]) * gain
        square = square + jnp.sum(val * val, axis=1, keepdims=True)
        cross = cross + jnp.sum(scaled * val, axis=1, keepdims=True)
        values.append(val)
        scaleds.append(scaled)
    rstd = lax.rsqrt(square * (1.0 / 4096) + 1e-05)
    inner = cross * rstd * (1.0 / 4096)
    a0_copies = [
        rc(gq0.at[1], G0.at[0, xh, c], a0_s.at[0], a0_r.at[0], sib),
        rc(gq1, G1.at[0, xh, c], a0_s.at[1], a0_r.at[1], sib),
        rc(gq0.at[0], G0.at[0, xh, c], a0_s.at[2], a0_r.at[2], opp),
        rc(gq0.at[1], G0.at[0, xh, c], a0_s.at[3], a0_r.at[3], opx),
    ]
    for (cc, t), val, scaled in zip(blocks, values, scaleds):
        back = (f32(grv[cc, :, SPAN[t]]) + rstd * (scaled - val * rstd * inner)).astype(BF16)
        if t == 1 and cc is oc:
            gq1[...] = back
            a0_copies[1].start()
        elif t == 1:
            G1[0, xh, c] = back
        elif cc is oc:
            gq0[1] = back
            a0_copies[3].start()
            a0_copies[0].start()
        else:
            gq0[0] = back
            a0_copies[2].start()
            G0[0, xh, c] = back

    outs = []

    def emit(src, dst):
        cp = pltpu.make_async_copy(src, dst, od.at[len(outs)])
        outs.append(cp)
        cp.start()

    def ag_copy(k, p, j):
        if j == 2:
            src, dst = G1.at[k, xh, p], G1.at[k + 1, xh, p]
        else:
            h = (xh, oh)[j]
            src, dst = G0.at[k, h, p], G0.at[k + 1, h, p]
        return rc(src, dst, ag_s.at[k, p, j], ag_r.at[k, p, j], nxt[p])

    def xf_copy(g, p):
        return rc(G1.at[g, xh, p], G1.at[g, xh, p], xf_s.at[g, p], xf_r.at[g, p], opp)

    def lead(k, last=False):
        for p in range(2):
            ag_copy(k, p, 2).wait_recv()
            if not last:
                ag_copy(k + 1, p, 2).start()
            xf_copy(k + 1, p).start()

    a0_copies[1].wait_recv()
    for p in range(2):
        ag_copy(0, p, 2).start()
        xf_copy(0, p).start()
    a0_copies[0].wait_recv()
    for p in range(2):
        ag_copy(0, p, 0).start()
    gwacc[...] = jnp.zeros_like(gwacc)
    dkacc[...] = jnp.zeros_like(dkacc)
    dvacc[...] = jnp.zeros_like(dvacc)
    a0_copies[2].wait_recv()
    a0_copies[3].wait_recv()
    for p in range(2):
        ag_copy(0, p, 1).start()
    lead(0)
    for e in range(2):
        emit(hidv.at[e], hid_out.at[:, e * 2048 : (e + 1) * 2048])
    emit(ngv, ng_out)
    emit(nmov, nmo_out)

    def weigh(g, last=False):
        for p in range(2):
            xf_copy(g, p).wait_recv()
        cx = both(g)
        gc = None
        for t, G in enumerate((G0, G1)):
            piece = dot_nt(G[g].reshape(4 * R, -1), wp[:, :, SPAN[t]].reshape(256, -1))
            gc = piece if gc is None else gc + piece
        gco[g] = gc[:, :HEAD]
        gcs[g] = gc[:, HEAD:]
        gc_copy(g).start()
        for t, G in enumerate((G0, G1)):
            total = gwacc[:, SPAN[t]] + dot_tn(cx, G[g].reshape(4 * R, -1))
            if last:
                gws[:, SPAN[t]] = total[HEAD:].astype(BF16)
                gwo[:, SPAN[t]] = total[:HEAD].astype(BF16)
            else:
                gwacc[:, SPAN[t]] = total

    def gc_copy(g):
        return rc(gcs.at[g], gcr.at[g], gc_s.at[g], gc_r.at[g], sib)

    def attend_back(g):
        gc_copy(g).wait_recv()
        s0, s1 = places(g)
        gc = (gco[g] + gcr[g]).astype(BF16)
        probs = prs[g]
        row_dot = jnp.sum(f32(gc) * f32(ctx[g, 0]), axis=1, keepdims=True)
        gs = (f32(probs) * (dot_nt(gc, vv[...]) - row_dot)).astype(BF16)
        dq = (dot(gs, kv[...]) * SCALE).astype(BF16)
        for h in range(2):
            for p, s in enumerate((s0, s1)):
                dqv[h, s, p] = dq[(2 * h + p) * R : (2 * h + p + 1) * R]
        dkacc[...] += dot_tn(gs, qs[g])
        dvacc[...] += dot_tn(probs, gc)

    def follow(k):
        for j in range(2):
            for p in range(2):
                ag_copy(k, p, j).wait_recv()
                ag_copy(k + 1, p, j).start()

    def backward(k, carry):
        follow(k)

        @pl.when(k < 5)
        def _():
            lead(k + 1)

        @pl.when(k == 5)
        def _():
            lead(6, last=True)

        weigh(k)

        @pl.when(k >= 1)
        def _():
            attend_back(k - 1)

        @pl.when(k == 1)
        def _():
            outer_d()

        return carry

    lax.fori_loop(0, 6, backward, 0)
    weigh(6)
    attend_back(5)
    for cp in id_copies:
        cp.wait_recv()
    for i in range(8):
        emit(pbuf.at[i // 2, i % 2], par_out.at[:, i * 512 : (i + 1) * 512])
    attend_back(6)
    for j in range(2):
        for p in range(2):
            ag_copy(6, p, j).wait_recv()
    weigh(7, last=True)
    gw_copy = rc(gws, gw_out.at[c], gw_s, gw_r, sib)
    gw_copy.start()
    emit(gwo, gw_out.at[c])
    attend_back(7)
    emit(dqv, dq_out)
    dkv[...] = (dkacc[...] * SCALE).astype(BF16)
    emit(dkv, dk_out)
    dvv[...] = dvacc[...].astype(BF16)
    emit(dvv, dv_out)

    w_copy.wait_send()
    gw_copy.wait_send()
    for cp in a_copies + fin_copies + a0_copies + id_copies + [ib_copy, ic_copy]:
        cp.wait_send()

    def drain8(g, carry):
        ctx_copy(g).wait_send()
        xe_copy(g).wait_send()
        gc_copy(g).wait_send()
        for p in range(2):
            xf_copy(g, p).wait_send()
        return carry

    lax.fori_loop(0, 8, drain8, 0)

    def drain7(k, carry):
        for p in range(2):
            for j in range(3):
                ring_copy(k, p, j).wait_send()
                ag_copy(k, p, j).wait_send()
        return carry

    lax.fori_loop(0, 7, drain7, 0)
    gw_copy.wait_recv()
    for cp in outs:
        cp.wait()


def finish(
    hid_in, dq_in, dk_in, dv_in, ng_in, nmo_in, par_in, gw_in, w_in, m1_in, m2_in,
    hid_out, dq_out, dk_out, dv_out, nw_out, nm1_out, nm2_out, ng_out, nmo_out, par_out,
    gw, w, m1, m2, par, hid, dq, dk, dv, ng, nmo, ld, od,
):
    outs, loads = [], []

    def emit(src, dst):
        cp = pltpu.make_async_copy(src, dst, od.at[len(outs)])
        outs.append(cp)
        cp.start()

    def load(src, dst):
        cp = pltpu.make_async_copy(src, dst, ld.at[len(loads)])
        loads.append(cp)
        cp.start()

    for i in range(4):
        rows = slice(i * 32, (i + 1) * 32)
        for e in range(2):
            load(gw_in.at[e, rows], gw.at[e, rows])
        load(m1_in.at[rows], m1.at[rows])
        load(m2_in.at[rows], m2.at[rows])
        load(w_in.at[rows], w.at[rows])
    passed = (
        (hid_in, hid, hid_out), (dq_in, dq, dq_out), (dk_in, dk, dk_out), (dv_in, dv, dv_out),
        (ng_in, ng, ng_out), (nmo_in, nmo, nmo_out), (par_in, par, par_out),
    )
    for src, mid, _ in passed:
        load(src, mid)
    for i in range(4):
        for cp in loads[5 * i : 5 * i + 5]:
            cp.wait()
        for rows in (slice(i * 32, i * 32 + 16), slice(i * 32 + 16, i * 32 + 32)):
            for e in range(2):
                at = slice(e * 2048, (e + 1) * 2048)
                grad = f32(gw[e, rows])
                first = 0.9 * f32(m1[rows, at]) + 0.1 * grad
                second = 0.95 * f32(m2[rows, at]) + 0.05 * grad * grad
                update = (first * (1.0 / (1.0 - 0.9**10))) / (
                    jnp.sqrt(second * (1.0 / (1.0 - 0.95**10))) + 1e-08
                )
                w[rows, at] = (f32(w[rows, at]) - 0.001 * update).astype(BF16)
                m1[rows, at] = first.astype(BF16)
                m2[rows, at] = second.astype(BF16)
        rows = slice(i * 32, (i + 1) * 32)
        for src, dst in ((w, nw_out), (m1, nm1_out), (m2, nm2_out)):
            emit(src.at[rows], dst.at[rows])
        for at in (2 * i, 2 * i + 1):
            if at < len(passed):
                loads[20 + at].wait()
                emit(passed[at][1], passed[at][2])
    for cp in outs:
        cp.wait()


def per_device(
    query, key, value, resid, w_out, gain, grad_norm, grad_resid, moment_one, moment_two,
    delta, global_w, momentum,
):
    any_spec = pl.BlockSpec(memory_space=pl.ANY)
    dma = pltpu.SemaphoreType.DMA

    def vm(shape, dtype=BF16):
        return pltpu.VMEM(shape, dtype)

    def shape(dims, dtype=BF16):
        return jax.ShapeDtypeStruct(dims, dtype)

    scratch = [
        vm((2, 8, 2, R, HEAD)), vm((1024, HEAD)), vm((1024, HEAD)),
        vm((2, 128, 2048)), vm((2, R, 2048)), vm((2, R, 2048)), vm((2, R, 2048)),
        vm((128, 512), F32), vm((128, 512), F32),
        vm((8, 128, HEAD)), vm((8, 128, 1024)), vm((8, 2, 128, HEAD)),
        vm((8, 2, 2, R, QZ)), vm((8, 2, 2, R, QX)), vm((8, 2, R, QX)),
        vm((7, 2, 2, R, QZ)), vm((7, 2, R, QX)),
        vm((2, 2, R, QZ)), vm((2, R, QX)), vm((3, R, QZ)), vm((R, QX)),
        vm((2, R, QZ)), vm((R, QX)), vm((8, 2, 2, R, QZ)), vm((8, 2, 2, R, QX)),
        vm((8, 128, HEAD), F32), vm((8, 128, HEAD), F32), vm((8, 128, HEAD), F32),
        vm((256, 2048), F32), vm((128, 2048)), vm((128, 2048)),
        vm((1024, HEAD), F32), vm((1024, HEAD), F32),
        vm((4, 2, 128, 512)), vm((128, 512)), vm((128, 512)),
        vm((2, R, 2048)), vm((2, 8, 2, R, HEAD)), vm((1024, HEAD)), vm((1024, HEAD)),
        vm((128, 512), F32), vm((128, 512), F32), vm((4, 2, 128, 512)),
        dma((14,)), dma((16,)), dma((8,)), dma((8,)), dma, dma,
        dma((8,)), dma((8,)), dma((7, 2, 3)), dma((7, 2, 3)),
        dma((4,)), dma((4,)), dma((4,)), dma((4,)),
        dma((7, 2, 3)), dma((7, 2, 3)), dma((8, 2)), dma((8, 2)),
        dma((8,)), dma((8,)), dma, dma,
        dma((3, 2)), dma((3, 2)), dma, dma, dma, dma, dma((3,)), dma((3,)),
    ]
    hidden, dq, dk, dv, ng, nmo, par, gw = pl.pallas_call(
        kernel,
        out_shape=[
            shape((R, 4096)), shape((2, 8, 2, R, HEAD)), shape((1024, HEAD)), shape((1024, HEAD)),
            shape((128, 512), F32), shape((128, 512), F32), shape((128, 4096)), shape((2, 128, 2048)),
        ],
        in_specs=[any_spec] * 5 + [pl.BlockSpec(memory_space=pltpu.VMEM)] + [any_spec] * 5,
        out_specs=[any_spec] * 8,
        scratch_shapes=scratch,
        compiler_params=pltpu.CompilerParams(
            collective_id=0, has_side_effects=True, vmem_limit_bytes=58 << 20
        ),
        cost_estimate=pl.CostEstimate(flops=5 * 10**9, bytes_accessed=12 << 20, transcendentals=10**6),
        name="whole_step",
    )(
        query.reshape(2, 8, 2, R, HEAD), key, value, resid, w_out[0], gain, grad_norm, grad_resid,
        delta[0], global_w, momentum,
    )
    hidden, dq, dk, dv, nw, nm1, nm2, ng, nmo, par = pl.pallas_call(
        finish,
        out_shape=[
            shape((R, 4096)), shape((2, 8, 2, R, HEAD)), shape((1024, HEAD)), shape((1024, HEAD)),
            shape((128, 4096)), shape((128, 4096)), shape((128, 4096)),
            shape((128, 512), F32), shape((128, 512), F32), shape((128, 4096)),
        ],
        in_specs=[any_spec] * 11,
        out_specs=[any_spec] * 10,
        scratch_shapes=[
            vm((2, 128, 2048)), vm((128, 4096)), vm((128, 4096)), vm((128, 4096)),
            vm((128, 4096)), vm((R, 4096)), vm((2, 8, 2, R, HEAD)), vm((1024, HEAD)), vm((1024, HEAD)),
            vm((128, 512), F32), vm((128, 512), F32), dma((27,)), dma((19,)),
        ],
        compiler_params=pltpu.CompilerParams(vmem_limit_bytes=58 << 20),
        cost_estimate=pl.CostEstimate(flops=10**7, bytes_accessed=12 << 20, transcendentals=10**6),
        name="finish",
    )(hidden, dq, dk, dv, ng, nmo, par, gw, w_out[0], moment_one[0], moment_two[0])
    return (
        hidden, dq.reshape(1024, HEAD), dk, dv, nw[None], nm1[None], nm2[None], ng, nmo, par,
    )


def solution(mesh):
    return jax.shard_map(
        per_device,
        mesh=mesh,
        in_specs=(
            P("island", "tp"),
            P("island", "tp"),
            P("island", "tp"),
            P(("island", "tp"), None),
            P("island", "tp", None),
            P("island", None),
            P(("island", "tp"), None),
            P(("island", "tp"), None),
            P("island", "tp", None),
            P("island", "tp", None),
            P("island", "tp", None),
            P("tp", "island"),
            P("tp", "island"),
        ),
        out_specs=(
            P(("island", "tp"), None),
            P("island", "tp"),
            P("island", "tp"),
            P("island", "tp"),
            P("island", "tp", None),
            P("island", "tp", None),
            P("island", "tp", None),
            P("tp", "island"),
            P("tp", "island"),
            P("tp", None),
        ),
        check_vma=False,
    )
```

time: 116 us -> 99.5 us (0.86)
  local copies, waits for them, and re-layouts: 12.2 us -> 0 us
  Pallas kernels: 102 us -> 98.5 us
    unnamed x26 -> x0, local copies, waits for them, and re-layouts: 12.2 us -> none
    pallas_call x1, Pallas kernels: 102 us -> 92.9 us  [per_device(): pl.pallas_call(kernel, out_shape=[shape((R, 4096)), shape((2, 8, 2, R, HE...]
    pallas_call x0 -> x1, Pallas kernels: none -> 5.58 us  [per_device(): pl.pallas_call(finish, out_shape=[shape((R, 4096)), shape((2, 8, 2, R, HE...]
where the time goes in v2:
time: 99.5 us; the launch traced here: 99.3 us
  Pallas kernels  98.5 us (99%)
    pallas_call x1, Pallas kernels, per_device(): pl.pallas_call(kernel, out_shape=[shape((R, 4096)), shape((2, 8, 2, R, HE...  92.9 us
    pallas_call x1, Pallas kernels, per_device(): pl.pallas_call(finish, out_shape=[shape((R, 4096)), shape((2, 8, 2, R, HE...  5.58 us

profile of v2, /device:TPU:1, one launch (start us, length us, event | category | flops | bytes accessed | tf_op | source)
XLA Modules:
  0.0 99.3 jit_solution(17089993661239887106)
XLA Ops:
  0.6 92.9 %whole_step.1 = (bf16[32,4096]{1,0:T(8,128)(2,1)}, bf16[2,8,2,32,128]{4,3,2,1,0:T(8,128)(2,1)}, bf16[1024,128]{1,0:T(8,128)(2,1)}, bf16[1024,128]{1,0:T(8,128)(2...) custom-call(bf16[2,8,2,32,128]{4,3,2,1,0:T(8,128)(2,1)} %bitcast.17, ...), custom_call_target="tpu_custom_call" | custom-call | flops 5000000000 | bytes 12582912 | tf_op jit(solution)/shard_map/whole_step/pallas_call | solution.py:585
  93.6 5.6 %finish.1 = (bf16[32,4096]{1,0:T(8,128)(2,1)}, bf16[2,8,2,32,128]{4,3,2,1,0:T(8,128)(2,1)}, bf16[1024,128]{1,0:T(8,128)(2,1)}, bf16[1024,128]{1,0:T(8,128)(2,1)}...) custom-call(bf16[32,4096]{1,0:T(8,128)(2,1)} %get-tuple-element.28.h, ...), custom_call_target="tpu_custom_call" | custom-call | flops 10000000 | bytes 12582912 | tf_op jit(solution)/shard_map/finish/pallas_call | solution.py:603

commit v3 on v2

--- a/solution.py
+++ b/solution.py
@@ -138,14 +138,13 @@
             src, dst = part1.at[k + 1, xh, p], rbuf1.at[k, p]
         return rc(src, dst, ring_s.at[k, p, j], ring_r.at[k, p, j], nxt[p])
 
-    def z_step(k, first=False):
-        for j in range(2):
-            h = halves[j]
-            for p in range(2):
-                if not first:
-                    ring_copy(k - 1, p, j).wait_recv()
-                    part0[k + 1, h, p] = (f32(part0[k + 1, h, p]) + f32(rbuf0[k - 1, p, j])).astype(BF16)
-                ring_copy(k, p, j).start()
+    def z_step(k, j, first=False):
+        h = halves[j]
+        for p in range(2):
+            if not first:
+                ring_copy(k - 1, p, j).wait_recv()
+                part0[k + 1, h, p] = (f32(part0[k + 1, h, p]) + f32(rbuf0[k - 1, p, j])).astype(BF16)
+            ring_copy(k, p, j).start()
 
     def x_step(k, first=False):
         xe_copy(k + 1).wait_recv()
@@ -217,24 +216,37 @@
     loads["wp"].wait()
     w_copy.wait_recv()
     project(1, order=(0, 1))
-    z_step(0, first=True)
+    z_step(0, 0, first=True)
+    z_step(0, 1, first=True)
     attend(3)
     ctx_copy(3).start()
     project(2)
+    attend(4)
+    ctx_copy(4).start()
     project(3)
 
-    def forward_step(k, second=False):
-        g = lax.rem(k + 3, NZ)
-        z_step(k)
-        attend(g)
-        ctx_copy(g).start()
-        x_step(k - 1, first=second)
-        project(g)
-
-    forward_step(1, second=True)
+    z_step(1, 0)
+    attend(5)
+    ctx_copy(5).start()
+    z_step(1, 1)
+    x_step(0, first=True)
+    project(4)
 
     def forward(k, carry):
-        forward_step(k)
+        z_step(k, 0)
+
+        @pl.when(k <= 4)
+        def _():
+            g = lax.rem(k + 4, NZ)
+            attend(g)
+            ctx_copy(g).start()
+
+        z_step(k, 1)
+        x_step(k - 1)
+
+        @pl.when(k <= 5)
+        def _():
+            project(lax.rem(k + 3, NZ))
 
         @pl.when(k == 3)
         def _():
@@ -246,9 +258,7 @@
 
         return carry
 
-    lax.fori_loop(2, 6, forward, 0)
-    z_step(6)
-    x_step(5)
+    lax.fori_loop(2, 7, forward, 0)
 
     fin_copies = [
         rc(zbuf.at[xh, oc], fin0.at[0], fin_s.at[0], fin_r.at[0], sib),
@@ -412,14 +422,22 @@
         dkacc[...] += dot_tn(gs, qs[g])
         dvacc[...] += dot_tn(probs, gc)
 
-    def follow(k):
-        for j in range(2):
-            for p in range(2):
-                ag_copy(k, p, j).wait_recv()
-                ag_copy(k + 1, p, j).start()
+    def follow(k, j):
+        for p in range(2):
+            ag_copy(k, p, j).wait_recv()
+            ag_copy(k + 1, p, j).start()
+
+    def drain(k):
+        for p in range(2):
+            for j in range(3):
+                ring_copy(k, p, j).wait_send()
+        ctx_copy(k).wait_send()
+        xe_copy(k).wait_send()
 
     def backward(k, carry):
-        follow(k)
+        follow(k, 0)
+        weigh(k)
+        follow(k, 1)
 
         @pl.when(k < 5)
         def _():
@@ -429,8 +447,6 @@
         def _():
             lead(6, last=True)
 
-        weigh(k)
-
         @pl.when(k >= 1)
         def _():
             attend_back(k - 1)
@@ -439,6 +455,7 @@
         def _():
             outer_d()
 
+        drain(k)
         return carry
 
     lax.fori_loop(0, 6, backward, 0)
@@ -449,6 +466,22 @@
     for i in range(8):
         emit(pbuf.at[i // 2, i % 2], par_out.at[:, i * 512 : (i + 1) * 512])
     attend_back(6)
+    drain(6)
+    ctx_copy(7).wait_send()
+    xe_copy(7).wait_send()
+    w_copy.wait_send()
+    for cp in a_copies + fin_copies + a0_copies + id_copies + [ib_copy, ic_copy]:
+        cp.wait_send()
+
+    def drain_back(k, carry):
+        for p in range(2):
+            for j in range(3):
+                ag_copy(k, p, j).wait_send()
+            xf_copy(k, p).wait_send()
+        gc_copy(k).wait_send()
+        return carry
+
+    lax.fori_loop(0, 6, drain_back, 0)
     for j in range(2):
         for p in range(2):
             ag_copy(6, p, j).wait_recv()
@@ -463,29 +496,11 @@
     dvv[...] = dvacc[...].astype(BF16)
     emit(dvv, dv_out)
 
-    w_copy.wait_send()
+    drain_back(6, 0)
+    for p in range(2):
+        xf_copy(7, p).wait_send()
+    gc_copy(7).wait_send()
     gw_copy.wait_send()
-    for cp in a_copies + fin_copies + a0_copies + id_copies + [ib_copy, ic_copy]:
-        cp.wait_send()
-
-    def drain8(g, carry):
-        ctx_copy(g).wait_send()
-        xe_copy(g).wait_send()
-        gc_copy(g).wait_send()
-        for p in range(2):
-            xf_copy(g, p).wait_send()
-        return carry
-
-    lax.fori_loop(0, 8, drain8, 0)
-
-    def drain7(k, carry):
-        for p in range(2):
-            for j in range(3):
-                ring_copy(k, p, j).wait_send()
-                ag_copy(k, p, j).wait_send()
-        return carry
-
-    lax.fori_loop(0, 7, drain7, 0)
     gw_copy.wait_recv()
     for cp in outs:
         cp.wait()

time: 99.5 us -> 98.3 us (0.988)
  Pallas kernels: 98.5 us -> 97.3 us
    pallas_call x1, Pallas kernels: 92.9 us -> 91.8 us  [per_device(): pl.pallas_call(kernel, out_shape=[shape((R, 4096)), shape((2, 8, 2, R, HE...]
where the time goes in v3:
time: 98.3 us; the launch traced here: 98.2 us
  Pallas kernels  97.3 us (99%)
    pallas_call x1, Pallas kernels, per_device(): pl.pallas_call(kernel, out_shape=[shape((R, 4096)), shape((2, 8, 2, R, HE...  91.8 us
    pallas_call x1, Pallas kernels, per_device(): pl.pallas_call(finish, out_shape=[shape((R, 4096)), shape((2, 8, 2, R, HE...  5.58 us

profile of v3, /device:TPU:1, one launch (start us, length us, event | category | flops | bytes accessed | tf_op | source)
XLA Modules:
  0.0 98.2 jit_solution(6111655101809409173)
XLA Ops:
  0.6 91.8 %whole_step.1 = (bf16[32,4096]{1,0:T(8,128)(2,1)}, bf16[2,8,2,32,128]{4,3,2,1,0:T(8,128)(2,1)}, bf16[1024,128]{1,0:T(8,128)(2,1)}, bf16[1024,128]{1,0:T(8,128)(2...) custom-call(bf16[2,8,2,32,128]{4,3,2,1,0:T(8,128)(2,1)} %bitcast.17, ...), custom_call_target="tpu_custom_call" | custom-call | flops 5000000000 | bytes 12582912 | tf_op jit(solution)/shard_map/whole_step/pallas_call | solution.py:600
  92.4 5.6 %finish.1 = (bf16[32,4096]{1,0:T(8,128)(2,1)}, bf16[2,8,2,32,128]{4,3,2,1,0:T(8,128)(2,1)}, bf16[1024,128]{1,0:T(8,128)(2,1)}, bf16[1024,128]{1,0:T(8,128)(2,1)}...) custom-call(bf16[32,4096]{1,0:T(8,128)(2,1)} %get-tuple-element.28.h, ...), custom_call_target="tpu_custom_call" | custom-call | flops 10000000 | bytes 12582912 | tf_op jit(solution)/shard_map/finish/pallas_call | solution.py:618
